TPU v7x, 32 devices: a whole 2x2x4 slice. The times are simulated.
32 devices in a mesh: gx: 8 (over z, x), gy: 4 (over y, core).
Axes of the slice: x: 2, y: 2, z: 4, core: 2. Of those that a mesh axis runs over, the one named last changes fastest.
Arguments:
- features: bfloat16 [16384, 128], P(('gx', 'gy')), may hold values from -6 to 6
- cotangent: bfloat16 [16384, 128], P(('gx', 'gy')), may hold values from -6 to 6
- block_pos: int32 [256], P(('gx', 'gy')), may hold values from -1 to 11, as said below
- weight_one: bfloat16 [3456, 128], replicated, may hold values from -0.1875 to 0.1875
- weight_two: bfloat16 [3456, 128], replicated, may hold values from -0.1875 to 0.1875
Outputs:
- output: bfloat16 [16384, 128], P(('gx', 'gy'))
- input_grad: float32 [16384, 128], P(('gx', 'gy'))
- grad_one: float32 [3456, 128], replicated
- grad_two: float32 [3456, 128], replicated
Inputs may be any that keep to these rules, and one draw needn't show every extreme that they name: `block_pos`: local position p numbers a device's 2 x 2 x 3 block grid as (bx * 2 + by) * 3 + bz. A device's used slots come first and hold distinct positions, the rest hold -1; every device uses 2 or more slots and some device uses all 8.
All inputs are finite; a program needn't handle non-finite values.
Results may differ from a plain program's by a relative error of at most 0.0043.
Values may be sent and summed in bfloat16 or wider, within the bound.
A program may use at most 128 MiB of HBM per device.

v0:
```python
import functools

import jax
import jax.numpy as jnp
import numpy as np
from jax import lax
from jax.experimental import pallas as pl
from jax.experimental.pallas import tpu as pltpu
from jax.sharding import PartitionSpec as P

PLANE = 96
GRID = 768
EXT = 960
C = 128
TAPS = 9 * C
MESH = pl.DeviceIdType.MESH
BF = jnp.bfloat16
F32 = jnp.float32


def dot(a, b):
    return jnp.dot(a, b, preferred_element_type=F32)


def dot_nt(a, b):
    return lax.dot_general(a, b, (((1,), (1,)), ((), ())), preferred_element_type=F32)


def kernel(n_gx, n_gy, rz, pos, feat, cot, w1_any, w2_any,
           out_ref, ig_ref, grad_ref,
           gp, yf, xr, yr, fx, fu, fh, fg, w1, w2, wt1, wt2, spread, acc, send_c, recv_c, s1b,
           recv_p, s2f, s2b, recv_z, gat,
           w_s, ex_s, ex_r, c_s, c_r, p_s, p_r, z_s, z_r, az_s, az_r, ap_s, ap_r, ac_s, ac_r):
    i = lax.axis_index("gx")
    j = lax.axis_index("gy")
    n3 = n_gx // 2
    ny = n_gy // 2
    np_ = 2 * ny
    half = acc.shape[1] // 2
    quarter = half // np_
    pad = rz * n3
    slots = feat.shape[0]
    core = lax.rem(j, 2)
    xb = lax.rem(i, 2)
    yb = j // 2
    me_p = yb * 2 + xb
    k = i // 2

    def shift(di, dj):
        return (lax.rem(i + di + n_gx, n_gx), lax.rem(j + dj + n_gy, n_gy))

    def plane_peer(r):
        rx, ry = r % 2, r // 2
        px = lax.rem(xb + rx, 2)
        py = lax.rem(yb + ry, ny)
        return (k * 2 + px, py * 2 + core), py * 2 + px

    def z_peer(d):
        pk = lax.rem(k + d, n3)
        return (pk * 2 + xb, j), pk

    other = (i, yb * 2 + (1 - core))
    dirs = [(a, b) for a in (-1, 0, 1) for b in (-1, 0, 1) if (a, b) != (0, 0)]

    barrier = pltpu.get_barrier_semaphore()
    targets = [shift(a, b) for a, b in dirs] + [other]
    targets += [plane_peer(r)[0] for r in range(1, np_)]
    targets += [z_peer(d)[0] for d in range(1, n3)]
    for t in targets:
        pl.semaphore_signal(barrier, inc=1, device_id=t, device_id_type=MESH)
    load_one = pltpu.make_async_copy(w1_any, w1, w_s.at[0])
    load_two = pltpu.make_async_copy(w2_any, w2, w_s.at[1])
    load_one.start()
    load_two.start()

    def remote(src, dst, ss, rs, dev):
        c = pltpu.make_async_remote_copy(src_ref=src, dst_ref=dst, send_sem=ss, recv_sem=rs,
                                         device_id=dev, device_id_type=MESH)
        c.start()
        return c

    def rows_at(shape, dim):
        row = lax.broadcasted_iota(jnp.int32, shape, dim)
        slot = row >> 6
        inner = ((row >> 4) & 3) * PLANE + (row & 3) * 8 + ((row >> 2) & 3)
        at = jnp.full(shape, -1, jnp.int32)
        for s in range(slots // 64):
            p = pos[s]
            third = (p * 86) >> 8
            corner = (third >> 1) * (4 * PLANE) + (p - 3 * third) * 32 + (third & 1) * 4
            corner = jnp.where(p >= 0, corner, -4 * GRID)
            at = jnp.where(slot == s, corner + inner, at)
        return at

    def one_hot(hit):
        return jnp.where(hit, 1.0, 0.0).astype(BF)

    place = one_hot(lax.broadcasted_iota(jnp.int32, (GRID, slots), 0) == rows_at((1, slots), 1))
    f_row = lax.broadcasted_iota(jnp.int32, (256, 1), 0)
    f_at = ((f_row >> 4) & 7) * PLANE + (f_row & 15) * 8 + (f_row >> 7) * 7
    f_at = jnp.where((f_row & 15) < 12, f_at, -1)
    face = one_hot(lax.broadcasted_iota(jnp.int32, (256, GRID), 1) == f_at)

    def put(f, a):
        gp[f] = a.astype(BF)
        yf[f] = dot(face, gp[f]).astype(BF)

    def exchange(e):
        copies = []
        for n, (a, b) in enumerate(dirs):
            if b == 0:
                src = gp.at[e, pl.ds(0 if a < 0 else GRID - PLANE, PLANE)]
                dst = xr.at[e, 1 if a < 0 else 0]
            else:
                base = 0 if b < 0 else 128
                side = 1 if b < 0 else 0
                if a == 0:
                    src = yf.at[e, pl.ds(base, 128)]
                    dst = yr.at[e, side, pl.ds(16, 128)]
                else:
                    src = yf.at[e, pl.ds(base + (0 if a < 0 else 112), 16)]
                    dst = yr.at[e, side, pl.ds(144 if a < 0 else 0, 16)]
            copies.append(remote(src, dst, ex_s.at[e, n], ex_r.at[e, n], shift(a, b)))
        return copies

    one = jnp.float32(1.0)
    zero = jnp.float32(0.0)
    lo_x = jnp.where(i > 0, one, zero)
    hi_x = jnp.where(i < n_gx - 1, one, zero)
    lo_y = jnp.where(j > 0, one, zero)
    hi_y = jnp.where(j < n_gy - 1, one, zero)

    def build(dst, e, copies):
        for c in copies:
            c.wait_recv()
        row = lax.broadcasted_iota(jnp.int32, (160, C), 0)
        edge = jnp.where(row < 16, lo_x, jnp.where(row >= 144, hi_x, one))
        ylo = dot(spread[0], (yr[e, 0].astype(F32) * (edge * lo_y)).astype(BF))
        yhi = dot(spread[1], (yr[e, 1].astype(F32) * (edge * hi_y)).astype(BF))
        xlo = xr[e, 0].astype(F32) * lo_x
        xhi = xr[e, 1].astype(F32) * hi_x
        ext = jnp.concatenate([xlo, gp[e].astype(F32), xhi], axis=0)
        ypos = lax.broadcasted_iota(jnp.int32, (EXT, C), 0) & 7
        below = jnp.where(ypos == 0, ylo, pltpu.roll(ext, 1, 0))
        above = jnp.where(ypos == 7, yhi, pltpu.roll(ext, EXT - 1, 0))
        blank = jnp.zeros((10, 8, C), F32)
        for dy, v in enumerate((below, ext, above)):
            v = v.reshape(10, PLANE, C)
            forms = (jnp.concatenate([blank, v[:, :PLANE - 8]], axis=1), v,
                     jnp.concatenate([v[:, 8:], blank], axis=1))
            for dz, w in enumerate(forms):
                o = (3 * dy + dz) * C
                dst[:, o:o + C] = w.reshape(EXT, C).astype(BF)

    def conv(f9, w):
        total = None
        for dx in range(3):
            t = dot(f9[dx * PLANE:dx * PLANE + GRID, :], w[dx * TAPS:(dx + 1) * TAPS, :])
            total = t if total is None else total + t
        return total

    def conv_t(f9, wt):
        total = None
        for dx in range(3):
            t = dot_nt(f9[dx * PLANE:dx * PLANE + GRID, :], wt[:, dx * TAPS:(dx + 1) * TAPS])
            total = t if total is None else total + t
        return total

    def core_start(g, left, f9):
        dx = g % 3
        t = dot(left, f9[dx * PLANE:dx * PLANE + GRID, :])
        for q in range(9):
            at = (8 - q if g < 3 else q) * C
            acc[g, at:at + C, :] = t[:, q * C:(q + 1) * C]
        send_c[g] = acc[g, pl.ds(pl.multiple_of((1 - core) * half, 16), half), :].astype(BF)
        return [remote(send_c.at[g], recv_c.at[g], c_s.at[g], c_r.at[g], other)]

    def plane_start(g):
        own = acc[g, pl.ds(pl.multiple_of(core * half, 16), half), :] + recv_c[g].astype(F32)
        s1b[g] = own.astype(BF)
        acc[g, pl.ds(pl.multiple_of(core * half, 16), half), :] = own
        copies = []
        for r in range(1, np_):
            dev, pq = plane_peer(r)
            copies.append(remote(s1b.at[g, pl.ds(pl.multiple_of(pq * quarter, 16), quarter)],
                                 recv_p.at[g, r - 1], p_s.at[g, r - 1], p_r.at[g, r - 1], dev))
        return copies

    def z_start(g):
        at = pl.multiple_of(core * half + me_p * quarter, 16)
        own = acc[g, pl.ds(at, quarter), :]
        for r in range(np_ - 1):
            own = own + recv_p[g, r].astype(F32)
        if pad > quarter:
            own = jnp.concatenate([own, jnp.zeros((pad - quarter, C), F32)], axis=0)
        s2f[g] = own
        s2b[g] = own.astype(BF)
        copies = []
        for d in range(1, n3):
            dev, pk = z_peer(d)
            copies.append(remote(s2b.at[g, pl.ds(pl.multiple_of(pk * rz, 16), rz)],
                                 recv_z.at[g, d - 1], z_s.at[g, d - 1], z_r.at[g, d - 1], dev))
        return copies

    def gather_z(g):
        own = s2f[g, pl.ds(pl.multiple_of(k * rz, 16), rz), :]
        for d in range(n3 - 1):
            own = own + recv_z[g, d].astype(F32)
        at = pl.multiple_of(k * rz, 16)
        gat[g, core * np_ + me_p, pl.ds(at, rz), :] = own.astype(BF)
        block = gat.at[g, core * np_ + me_p, pl.ds(at, rz)]
        return [remote(block, block, az_s.at[g, d - 1], az_r.at[g, d - 1], z_peer(d)[0])
                for d in range(1, n3)]

    def gather_plane(g):
        block = gat.at[g, core * np_ + me_p, pl.ds(0, quarter)]
        return [remote(block, block, ap_s.at[g, r - 1], ap_r.at[g, r - 1], plane_peer(r)[0])
                for r in range(1, np_)]

    def gather_core(g):
        block = gat.at[g, pl.ds(core * np_, np_), pl.ds(0, quarter)]
        return [remote(block, block, ac_s.at[g], ac_r.at[g], other)]

    def finish(g):
        if g < 3:
            first = (18 - 9 * g) * C
            for q in range(2 * np_):
                at = first + q * quarter
                grad_ref[0, at:at + quarter, :] = gat[g, q, 0:quarter, :]
        else:
            first = 9 * (g - 3) * C
            whole = jnp.concatenate([gat[g, q, 0:quarter, :] for q in range(2 * np_)], axis=0)
            for q in range(9):
                block = jnp.transpose(whole[q * C:(q + 1) * C, :].astype(F32))
                grad_ref[1, first + q * C:first + (q + 1) * C, :] = block.astype(BF)
        return []

    stages = (None, plane_start, z_start, gather_z, gather_plane, gather_core, finish)
    flight = {}
    pending = []

    def advance(*steps):
        for stage, g in steps:
            for c in flight[g]:
                c.wait_recv()
            flight[g] = stages[stage](g)
            pending.extend(flight[g])

    def begin(g, left, f9):
        flight[g] = core_start(g, left, f9)
        pending.extend(flight[g])

    xg = dot(place, feat[...])
    put(0, xg)
    pl.semaphore_wait(barrier, len(targets))
    ex_x = exchange(0)
    ug = dot(place, cot[...])
    put(1, ug)
    ex_u = exchange(1)
    mask = dot(place, jnp.ones((slots, C), BF))
    s_col = lax.broadcasted_iota(jnp.int32, (1, 160), 1)
    s_at = jnp.where((s_col & 15) < 12, (s_col >> 4) * PLANE + (s_col & 15) * 8, -8)
    s_row = lax.broadcasted_iota(jnp.int32, (EXT, 160), 0)
    spread[0] = one_hot(s_row == s_at)
    spread[1] = one_hot(s_row == s_at + 7)
    load_one.wait()
    load_two.wait()
    for o in range(27):
        lanes = slice(o * C, (o + 1) * C)
        rows = slice((26 - o) * C, (27 - o) * C)
        wt1[:, lanes] = w1[rows, :]
        wt2[:, lanes] = w2[rows, :]
    build(fx, 0, ex_x)
    pre = conv(fx, w1)
    sig = jax.nn.sigmoid(pre)
    hidden = pre * sig * mask
    h_t = jnp.transpose(hidden).astype(BF)
    build(fu, 1, ex_u)
    for g in range(3):
        begin(g, h_t, fu)
    put(2, hidden)
    advance((1, 0))
    back = conv_t(fu, wt2)
    hgrad = back * (sig * (1.0 + pre * (1.0 - sig))) * mask
    hg_t = jnp.transpose(hgrad).astype(BF)
    advance((1, 1), (1, 2))
    for g in range(3, 6):
        begin(g, hg_t, fx)
    put(3, hgrad)
    ex_h = exchange(2)
    advance((1, 3))
    ex_g = exchange(3)
    advance((2, 0), (1, 4), (1, 5), (2, 1))
    build(fh, 2, ex_h)
    advance((2, 2), (3, 0))
    pre_two = conv(fh, w2)
    advance((3, 1), (2, 3))
    pick = one_hot(lax.broadcasted_iota(jnp.int32, (slots, GRID), 1) == rows_at((slots, 1), 0))
    og = (pre_two + gp[0].astype(F32)).astype(BF)
    out_ref[...] = dot(pick, og).astype(BF)
    advance((3, 2), (4, 0), (2, 4))
    build(fg, 3, ex_g)
    advance((4, 1), (2, 5), (3, 3))
    ig = conv_t(fg, wt1) + gp[1].astype(F32)
    advance((4, 2), (3, 4), (5, 0), (3, 5))
    ig_hi = ig.astype(BF)
    ig_lo = (ig - ig_hi.astype(F32)).astype(BF)
    ig_ref[...] = dot(pick, ig_hi) + dot(pick, ig_lo)
    advance((4, 3), (5, 1), (4, 4), (5, 2), (4, 5), (6, 0), (6, 1), (6, 2), (5, 3), (5, 4), (5, 5),
            (6, 3), (6, 4), (6, 5))
    for c in ex_x + ex_u + ex_g + ex_h + pending:
        c.wait_send()


def finish_kernel(scale, parts, grads, out, ig, out_ref, ig_ref, one_ref, two_ref,
                  narrow, wide, side_out, side_ig, in_s, out_s, side_s):
    size = grads.shape[1] // parts
    chunks = [(g, q) for q in range(parts) for g in range(2)]
    loads = []
    for n, (g, q) in enumerate(chunks):
        loads.append(pltpu.make_async_copy(
            grads.at[g, pl.ds(q * size, size)], narrow.at[n], in_s.at[n]))
        loads[-1].start()
    sides = [pltpu.make_async_copy(out, side_out, side_s.at[0]),
             pltpu.make_async_copy(ig, side_ig, side_s.at[1])]
    for c in sides:
        c.start()
    ends = []
    for n, (g, q) in enumerate(chunks):
        loads[n].wait()
        wide[n] = narrow[n].astype(F32) * scale
        to = one_ref if g else two_ref
        ends.append(pltpu.make_async_copy(wide.at[n], to.at[pl.ds(q * size, size)], out_s.at[n]))
        ends[-1].start()
    backs = [pltpu.make_async_copy(side_out, out_ref, side_s.at[2]),
             pltpu.make_async_copy(side_ig, ig_ref, side_s.at[3])]
    for a, b in zip(sides, backs):
        a.wait()
        b.start()
    for c in ends + backs:
        c.wait()


def per_device(n_gx, n_gy, features, cotangent, block_pos, weight_one, weight_two):
    rows = features.shape[0]
    n3 = n_gx // 2
    np_ = n_gy
    taps = weight_one.shape[0]
    group = taps // 3
    half = group // 2
    quarter = half // np_
    rz = -(-quarter // (16 * n3)) * 16
    pad = rz * n3
    vm = pl.BlockSpec(memory_space=pltpu.VMEM)
    dma = pltpu.SemaphoreType.DMA
    out, ig, grads = pl.pallas_call(
        functools.partial(kernel, n_gx, n_gy, rz),
        out_shape=(jax.ShapeDtypeStruct((rows, C), BF), jax.ShapeDtypeStruct((rows, C), F32),
                   jax.ShapeDtypeStruct((2, taps, C), BF)),
        in_specs=[pl.BlockSpec(memory_space=pltpu.SMEM), vm, vm,
                  pl.BlockSpec(memory_space=pl.ANY), pl.BlockSpec(memory_space=pl.ANY)],
        out_specs=(vm, vm, vm),
        scratch_shapes=[
            pltpu.VMEM((4, GRID, C), BF),
            pltpu.VMEM((4, 256, C), BF),
            pltpu.VMEM((4, 2, PLANE, C), BF),
            pltpu.VMEM((4, 2, 160, C), BF),
            pltpu.VMEM((EXT, TAPS), BF),
            pltpu.VMEM((EXT, TAPS), BF),
            pltpu.VMEM((EXT, TAPS), BF),
            pltpu.VMEM((EXT, TAPS), BF),
            pltpu.VMEM((taps, C), BF),
            pltpu.VMEM((taps, C), BF),
            pltpu.VMEM((C, taps), BF),
            pltpu.VMEM((C, taps), BF),
            pltpu.VMEM((2, EXT, 160), BF),
            pltpu.VMEM((6, group, C), F32),
            pltpu.VMEM((6, half, C), BF),
            pltpu.VMEM((6, half, C), BF),
            pltpu.VMEM((6, half, C), BF),
            pltpu.VMEM((6, np_ - 1, quarter, C), BF),
            pltpu.VMEM((6, pad, C), F32),
            pltpu.VMEM((6, pad, C), BF),
            pltpu.VMEM((6, n3 - 1, rz, C), BF),
            pltpu.VMEM((6, 2 * np_, pad, C), BF),
            dma((2,)),
            dma((4, 8)), dma((4, 8)),
            dma((6,)), dma((6,)),
            dma((6, np_ - 1)), dma((6, np_ - 1)),
            dma((6, n3 - 1)), dma((6, n3 - 1)),
            dma((6, n3 - 1)), dma((6, n3 - 1)),
            dma((6, np_ - 1)), dma((6, np_ - 1)),
            dma((6,)), dma((6,)),
        ],
        compiler_params=pltpu.CompilerParams(
            collective_id=0, has_side_effects=True, vmem_limit_bytes=56 * 1024 * 1024),
        cost_estimate=pl.CostEstimate(flops=5_000_000_000, bytes_accessed=8_000_000,
                                      transcendentals=200_000),
    )(block_pos, features, cotangent, weight_one, weight_two)
    scale = float(1.0 / np.sqrt(np.float32(rows * n_gx * n_gy)))
    parts = 6
    hbm = pl.BlockSpec(memory_space=pl.ANY)
    return tuple(pl.pallas_call(
        functools.partial(finish_kernel, scale, parts),
        out_shape=(jax.ShapeDtypeStruct((rows, C), BF), jax.ShapeDtypeStruct((rows, C), F32),
                   jax.ShapeDtypeStruct((taps, C), F32), jax.ShapeDtypeStruct((taps, C), F32)),
        in_specs=[hbm] * 3,
        out_specs=(hbm,) * 4,
        scratch_shapes=[
            pltpu.VMEM((2 * parts, taps // parts, C), BF),
            pltpu.VMEM((2 * parts, taps // parts, C), F32),
            pltpu.VMEM((rows, C), BF), pltpu.VMEM((rows, C), F32),
            dma((2 * parts,)), dma((2 * parts,)), dma((4,)),
        ],
        compiler_params=pltpu.CompilerParams(vmem_limit_bytes=56 * 1024 * 1024),
    )(grads, out, ig))


def solution(mesh):
    shape = dict(mesh.shape)
    in_specs = (P(("gx", "gy"), None), P(("gx", "gy"), None), P(("gx", "gy")), P(), P())
    out_specs = (P(("gx", "gy"), None), P(("gx", "gy"), None), P(), P())
    return jax.shard_map(
        functools.partial(per_device, shape["gx"], shape["gy"]),
        mesh=mesh, in_specs=in_specs, out_specs=out_specs, check_vma=False,
    )
```

profile of v0, /device:TPU:1, one launch (start us, length us, event | category | flops | bytes accessed | tf_op | source)
XLA Modules:
  0.0 53.0 jit_solution(13349474612370552966)
XLA Ops:
  0.6 49.1 %shard_map.84 = (bf16[512,128]{1,0:T(8,128)(2,1)}, f32[512,128]{1,0:T(8,128)}, bf16[2,3456,128]{2,1,0:T(8,128)(2,1)}) custom-call(s32[8]{0:T(128)} %pos.1, bf16[512,128]{1,0:T(8,128)(2,1)} %feat.1, bf16[512,128]{1,0:T(8,128)(2,1)} %cot.1, bf16[3456,128]{1,0:T(8,128)(2,1)} %w1_any.1, bf16[3456,128]{1,0:T(8,128)(2,1)} %w2_any.1), custom_call_target="tpu_custom_call" | custom-call | flops 5000000000 | bytes 8000000 | tf_op jit(solution)/shard_map/pallas_call | solution.py:356
  49.7 3.1 %shard_map.85 = (bf16[512,128]{1,0:T(8,128)(2,1)}, f32[512,128]{1,0:T(8,128)}, f32[3456,128]{1,0:T(8,128)}, f32[3456,128]{1,0:T(8,128)}) custom-call(bf16[2,3456,128]{2,1,0:T(8,128)(2,1)} %get-tuple-element.7.grads, bf16[512,128]{1,0:T(8,128)(2,1)} %get-tuple-element.8.out, f32[512,128]{1,0:T(8,128)} %get-tuple-element.9.ig), custom_call_target="tpu_custom_call" | custom-call | tf_op jit(solution)/shard_map/pallas_call | solution.py:403
where the time goes:
time: 53.1 us; the launch traced here: 53 us
  Pallas kernels  52.2 us (98%)
  between operations  0.8 us (2%)
    pallas_call x1, Pallas kernels, per_device(): pl.pallas_call(functools.partial(kernel, n_gx, n_gy, rz), out_shape=(jax....  49.1 us
    pallas_call x1, Pallas kernels, per_device(): pl.pallas_call(functools.partial(finish_kernel, scale, parts), out_shape=...  3.09 us

commit v1 on v0

--- a/solution.py
+++ b/solution.py
@@ -284,13 +284,15 @@
     hgrad = back * (sig * (1.0 + pre * (1.0 - sig))) * mask
     hg_t = jnp.transpose(hgrad).astype(BF)
     advance((1, 1), (1, 2))
-    for g in range(3, 6):
-        begin(g, hg_t, fx)
+    begin(3, hg_t, fx)
+    begin(4, hg_t, fx)
+    advance((1, 3))
+    begin(5, hg_t, fx)
+    advance((1, 4), (2, 0), (1, 5))
+    ex_h = exchange(2)
     put(3, hgrad)
-    ex_h = exchange(2)
-    advance((1, 3))
     ex_g = exchange(3)
-    advance((2, 0), (1, 4), (1, 5), (2, 1))
+    advance((2, 1))
     build(fh, 2, ex_h)
     advance((2, 2), (3, 0))
     pre_two = conv(fh, w2)

time: 53.1 us -> 58 us (1.092)
  Pallas kernels: 52.2 us -> 57.1 us
    pallas_call x1, Pallas kernels: 49.1 us -> 54 us  [per_device(): pl.pallas_call(functools.partial(kernel, n_gx, n_gy, rz), out_shape=(jax....]
where the time goes in v1:
time: 58 us; the launch traced here: 57.9 us
  Pallas kernels  57.1 us (98%)
  between operations  0.8 us (1%)
    pallas_call x1, Pallas kernels, per_device(): pl.pallas_call(functools.partial(kernel, n_gx, n_gy, rz), out_shape=(jax....  54 us
    pallas_call x1, Pallas kernels, per_device(): pl.pallas_call(functools.partial(finish_kernel, scale, parts), out_shape=...  3.09 us

profile of v1, /device:TPU:1, one launch (start us, length us, event | category | flops | bytes accessed | tf_op | source)
XLA Modules:
  0.0 57.9 jit_solution(11403887858866594609)
XLA Ops:
  0.6 54.0 %shard_map.84 = (bf16[512,128]{1,0:T(8,128)(2,1)}, f32[512,128]{1,0:T(8,128)}, bf16[2,3456,128]{2,1,0:T(8,128)(2,1)}) custom-call(s32[8]{0:T(128)} %pos.1, bf16[512,128]{1,0:T(8,128)(2,1)} %feat.1, bf16[512,128]{1,0:T(8,128)(2,1)} %cot.1, bf16[3456,128]{1,0:T(8,128)(2,1)} %w1_any.1, bf16[3456,128]{1,0:T(8,128)(2,1)} %w2_any.1), custom_call_target="tpu_custom_call" | custom-call | flops 5000000000 | bytes 8000000 | tf_op jit(solution)/shard_map/pallas_call | solution.py:358
  54.6 3.1 %shard_map.85 = (bf16[512,128]{1,0:T(8,128)(2,1)}, f32[512,128]{1,0:T(8,128)}, f32[3456,128]{1,0:T(8,128)}, f32[3456,128]{1,0:T(8,128)}) custom-call(bf16[2,3456,128]{2,1,0:T(8,128)(2,1)} %get-tuple-element.7.grads, bf16[512,128]{1,0:T(8,128)(2,1)} %get-tuple-element.8.out, f32[512,128]{1,0:T(8,128)} %get-tuple-element.9.ig), custom_call_target="tpu_custom_call" | custom-call | tf_op jit(solution)/shard_map/pallas_call | solution.py:405
